TPU v7x, 768 devices: a whole 4x8x12 slice. The times are simulated.
768 devices in a mesh: row: 32 (over z_hi, x, core), col: 24 (over z_lo, y).
Axes of the slice: x: 4, y: 8, z: 12 (z_hi: 4, z_lo: 3; z = z_hi * 3 + z_lo), core: 2. Of those that a mesh axis runs over, the one named last changes fastest.
Arguments:
- u_blocks: float32 [96, 168, 128, 128], P('row', 'col'), may hold values from -0.21875 to 0.21875
- u_rows: int32 [96, 168], P('row', 'col'), may hold values from 0 to 2
Outputs:
- squares: float32 [128, 72, 3, 128, 128], P('row', 'col')
All inputs are finite; a program needn't handle non-finite values.
Results may differ from a plain program's by a relative error of at most 0.0001.
Values sent between devices are 32-bit elements; how exact they have to be, the bound alone decides.
A program may use at most 32 MiB of HBM per device.

v0:
```python
import jax
import jax.numpy as jnp
from jax import lax
from jax.sharding import PartitionSpec as P

STEPS = 4


def passed_along(block, axis, distance):
    devices = range(lax.axis_size(axis))
    route = [((i - distance) % len(devices), i) for i in devices]
    return lax.ppermute(block, axis, route)


def one_hot(rows, count):
    return (rows[..., None] == jnp.arange(count, dtype=jnp.int32)).astype(jnp.float32)


def place_columns(hot_rows, blocks):
    return jnp.einsum("ki,kab->ikab", hot_rows, blocks, precision=lax.Precision.HIGHEST)


def place_transposed(hot_rows, blocks):
    return jnp.einsum("ik,iba->ikab", hot_rows, blocks, precision=lax.Precision.HIGHEST)


def block_product(left_side, right_side):
    return jnp.einsum("ikab,kjbc->ijac", left_side, right_side, precision=lax.Precision.HIGHEST)


def shards(u_blocks, u_rows):
    count = u_blocks.shape[0]
    onsite_hot = one_hot(u_rows[:, 0], count)
    onsite = place_columns(onsite_hot, u_blocks[:, 0]) + place_transposed(
        onsite_hot, u_blocks[:, 0]
    )
    results = [block_product(onsite, onsite)]
    for step in range(1, STEPS):
        forward = u_blocks[:, step]
        backward = u_blocks[:, step + STEPS - 1]
        forward_rows = u_rows[:, step]
        backward_rows = u_rows[:, step + STEPS - 1]
        halfway = passed_along((forward, backward, forward_rows, backward_rows), "row", -step)
        near_pair = passed_along((halfway[0], halfway[1], halfway[2], halfway[3]), "col", -step)
        far_backward, far_backward_rows = passed_along((backward, backward_rows), "col", -2 * step)
        far_forward, far_forward_rows = passed_along((forward, forward_rows), "row", -2 * step)
        left_side = place_columns(one_hot(near_pair[2], count), near_pair[0])
        left_side = left_side + place_transposed(one_hot(far_backward_rows, count), far_backward)
        right_side = place_columns(one_hot(far_forward_rows, count), far_forward)
        right_side = right_side + place_transposed(one_hot(near_pair[3], count), near_pair[1])
        results.append(block_product(left_side, right_side))
    return jnp.stack(results)


def solution(mesh):
    return jax.shard_map(
        shards,
        mesh=mesh,
        in_specs=(P("row", "col", None, None), P("row", "col")),
        out_specs=P("row", "col", None, None, None),
        check_vma=False,
    )
```

profile of v0, /device:TPU:40, one launch (start us, length us, event | category | flops | bytes accessed | tf_op | source)
XLA Modules:
  0.0 284.1 jit_solution(17735147427680939620)
XLA Ops:
  1.2 2.9 %collective-permute-start.22 = (s32[3]{0:T(128)S(1)}, s32[3]{0:T(128)S(1)}, u32[]{:S(2)}, u32[]{:S(2)}) collective-permute-start(s32[3]{0:T(128)S(1)} %get-tuple-element.6), channel_id=1, source_target_pairs={{4,0},{5,1},{6,2},{7,3},{8,4},{9,5},{10,6},{11,7},{12,8},{13,9},{1... | collective-permute-start | bytes 44 | tf_op jit(solution)/shard_map/ppermute | solution.py:12
  4.2 16.8 %collective-permute-start.14 = (s32[3]{0:T(128)S(1)}, s32[3]{0:T(128)S(1)}, u32[]{:S(2)}, u32[]{:S(2)}) collective-permute-start(s32[3]{0:T(128)S(1)} %get-tuple-element.6), channel_id=1, source_target_pairs={{48,0},{72,24},{96,48},{120,72},{144,96},{168,120},{192,144},{216,... | collective-permute-start | bytes 44 | tf_op jit(solution)/shard_map/ppermute | solution.py:12
  26.1 7.1 %collective-permute-start.10 = (s32[3]{0:T(128)S(1)}, s32[3]{0:T(128)S(1)}, u32[]{:S(2)}, u32[]{:S(2)}) collective-permute-start(s32[3]{0:T(128)S(1)} %get-tuple-element.8), channel_id=1, source_target_pairs={{2,0},{3,1},{4,2},{5,3},{6,4},{7,5},{8,6},{9,7},{10,8},{11,9},{12,... | collective-permute-start | bytes 44 | tf_op jit(solution)/shard_map/ppermute | solution.py:12
  36.5 4.5 %collective-permute-start.2 = (s32[3]{0:T(128)S(1)}, s32[3]{0:T(128)S(1)}, u32[]{:S(2)}, u32[]{:S(2)}) collective-permute-start(s32[3]{0:T(128)S(1)} %get-tuple-element.8), channel_id=1, source_target_pairs={{24,0},{48,24},{72,48},{96,72},{120,96},{144,120},{168,144},{192,1... | collective-permute-start | bytes 44 | tf_op jit(solution)/shard_map/ppermute | solution.py:12
  41.0 4.0 %collective-permute-start.6 = (s32[3]{0:T(128)S(1)}, s32[3]{0:T(128)S(1)}, u32[]{:S(2)}, u32[]{:S(2)}) collective-permute-start(s32[3]{0:T(128)S(1)} %get-tuple-element.9), channel_id=1, source_target_pairs={{24,0},{48,24},{72,48},{96,72},{120,96},{144,120},{168,144},{192,1... | collective-permute-start | bytes 44 | tf_op jit(solution)/shard_map/ppermute | solution.py:12
  47.3 3.2 %collective-permute-done = s32[3]{0:T(128)S(1)} collective-permute-done((s32[3]{0:T(128)S(1)}, s32[3]{0:T(128)S(1)}, u32[]{:S(2)}, u32[]{:S(2)}) %collective-permute-start) | collective-permute-done | bytes 44 | tf_op jit(solution)/shard_map/ppermute | solution.py:12
  52.5 6.4 %collective-permute-done.34 = s32[3]{0:T(128)S(1)} collective-permute-done((s32[3]{0:T(128)S(1)}, s32[3]{0:T(128)S(1)}, u32[]{:S(2)}, u32[]{:S(2)}) %collective-permute-start.34) | collective-permute-done | bytes 44 | tf_op jit(solution)/shard_map/ppermute | solution.py:12
  60.9 4.6 %collective-permute-done.24 = s32[3]{0:T(128)S(1)} collective-permute-done((s32[3]{0:T(128)S(1)}, s32[3]{0:T(128)S(1)}, u32[]{:S(2)}, u32[]{:S(2)}) %collective-permute-start.24) | collective-permute-done | bytes 44 | tf_op jit(solution)/shard_map/ppermute | solution.py:12
  67.6 3.5 %collective-permute-start.23 = (f32[3,128,128]{2,1,0:T(8,128)S(1)}, f32[3,128,128]{2,1,0:T(8,128)S(1)}, u32[]{:S(2)}, u32[]{:S(2)}) collective-permute-start(f32[3,128,128]{2,1,0:T(8,128)S(1)} %get-tuple-element.13), channel_id=1, source_target_pairs={{4,0},{5,1},{6,2},{7,3},{8,4},{9,5},{10,6},{11,7},{12,8},{13,9},{1... | collective-permute-start | bytes 589832 | tf_op jit(solution)/shard_map/ppermute | solution.py:12
  71.1 4.0 %collective-permute-start.15 = (s32[3]{0:T(128)S(1)}, s32[3]{0:T(128)S(1)}, u32[]{:S(2)}, u32[]{:S(2)}) collective-permute-start(s32[3]{0:T(128)S(1)} %collective-permute-done.14), channel_id=1, source_target_pairs={{2,0},{3,1},{4,2},{5,3},{6,4},{7,5},{8,6},{9,7},{10,8},{11,9},{12,... | collective-permute-start | bytes 44 | tf_op jit(solution)/shard_map/ppermute | solution.py:12
  77.4 5.4 %collective-permute-start.19 = (s32[3]{0:T(128)S(1)}, s32[3]{0:T(128)S(1)}, u32[]{:S(2)}, u32[]{:S(2)}) collective-permute-start(s32[3]{0:T(128)S(1)} %collective-permute-done.18), channel_id=1, source_target_pairs={{2,0},{3,1},{4,2},{5,3},{6,4},{7,5},{8,6},{9,7},{10,8},{11,9},{12,... | collective-permute-start | bytes 44 | tf_op jit(solution)/shard_map/ppermute | solution.py:12
  84.6 9.9 %collective-permute-start.16 = (f32[3,128,128]{2,1,0:T(8,128)S(1)}, f32[3,128,128]{2,1,0:T(8,128)}, u32[]{:S(2)}, u32[]{:S(2)}) collective-permute-start(f32[3,128,128]{2,1,0:T(8,128)S(1)} %get-tuple-element.13), channel_id=1, source_target_pairs={{48,0},{72,24},{96,48},{120,72},{144,96},{168,120},{192,144},{216,... | collective-permute-start | bytes 589832 | tf_op jit(solution)/shard_map/ppermute | solution.py:12
  96.5 4.0 %collective-permute-start.3 = (s32[3]{0:T(128)S(1)}, s32[3]{0:T(128)S(1)}, u32[]{:S(2)}, u32[]{:S(2)}) collective-permute-start(s32[3]{0:T(128)S(1)} %collective-permute-done.2), channel_id=1, source_target_pairs={{1,0},{2,1},{3,2},{4,3},{5,4},{6,5},{7,6},{8,7},{9,8},{10,9},{11,1... | collective-permute-start | bytes 44 | tf_op jit(solution)/shard_map/ppermute | solution.py:12
  100.5 5.1 %collective-permute-done.3 = s32[3]{0:T(128)S(1)} collective-permute-done((s32[3]{0:T(128)S(1)}, s32[3]{0:T(128)S(1)}, u32[]{:S(2)}, u32[]{:S(2)}) %collective-permute-start.3) | collective-permute-done | bytes 44 | tf_op jit(solution)/shard_map/ppermute | solution.py:12
  107.5 3.5 %collective-permute-done.7 = s32[3]{0:T(128)S(1)} collective-permute-done((s32[3]{0:T(128)S(1)}, s32[3]{0:T(128)S(1)}, u32[]{:S(2)}, u32[]{:S(2)}) %collective-permute-start.7) | collective-permute-done | bytes 44 | tf_op jit(solution)/shard_map/ppermute | solution.py:12
  111.0 3.4 %collective-permute-start.13 = (f32[3,128,128]{2,1,0:T(8,128)S(1)}, f32[3,128,128]{2,1,0:T(8,128)S(1)}, u32[]{:S(2)}, u32[]{:S(2)}) collective-permute-start(f32[3,128,128]{2,1,0:T(8,128)S(1)} %get-tuple-element.14), channel_id=1, source_target_pairs={{96,0},{120,24},{144,48},{168,72},{192,96},{216,120},{240,144},{26... | collective-permute-start | bytes 589832 | tf_op jit(solution)/shard_map/ppermute | solution.py:12
  116.3 16.1 %collective-permute-done.30 = s32[3]{0:T(128)S(1)} collective-permute-done((s32[3]{0:T(128)S(1)}, s32[3]{0:T(128)S(1)}, u32[]{:S(2)}, u32[]{:S(2)}) %collective-permute-start.30) | collective-permute-done | bytes 44 | tf_op jit(solution)/shard_map/ppermute | solution.py:12
  132.4 5.9 %collective-permute-start.27 = (s32[3]{0:T(128)S(1)}, s32[3]{0:T(128)S(1)}, u32[]{:S(2)}, u32[]{:S(2)}) collective-permute-start(s32[3]{0:T(128)S(1)} %collective-permute-done.26), channel_id=1, source_target_pairs={{3,0},{4,1},{5,2},{6,3},{7,4},{8,5},{9,6},{10,7},{11,8},{12,9},{13... | collective-permute-start | bytes 44 | tf_op jit(solution)/shard_map/ppermute | solution.py:12
  138.3 3.4 %collective-permute-done.27 = s32[3]{0:T(128)S(1)} collective-permute-done((s32[3]{0:T(128)S(1)}, s32[3]{0:T(128)S(1)}, u32[]{:S(2)}, u32[]{:S(2)}) %collective-permute-start.27) | collective-permute-done | bytes 44 | tf_op jit(solution)/shard_map/ppermute | solution.py:12
  141.7 5.0 %collective-permute-start.31 = (s32[3]{0:T(128)S(1)}, s32[3]{0:T(128)S(1)}, u32[]{:S(2)}, u32[]{:S(2)}) collective-permute-start(s32[3]{0:T(128)S(1)} %collective-permute-done.30), channel_id=1, source_target_pairs={{3,0},{4,1},{5,2},{6,3},{7,4},{8,5},{9,6},{10,7},{11,8},{12,9},{13... | collective-permute-start | bytes 44 | tf_op jit(solution)/shard_map/ppermute | solution.py:12
  146.7 4.3 %collective-permute-done.31 = s32[3]{0:T(128)S(1)} collective-permute-done((s32[3]{0:T(128)S(1)}, s32[3]{0:T(128)S(1)}, u32[]{:S(2)}, u32[]{:S(2)}) %collective-permute-start.31) | collective-permute-done | bytes 44 | tf_op jit(solution)/shard_map/ppermute | solution.py:12
  151.0 3.7 %collective-permute-start.11 = (f32[3,128,128]{2,1,0:T(8,128)S(1)}, f32[3,128,128]{2,1,0:T(8,128)S(1)}, u32[]{:S(2)}, u32[]{:S(2)}) collective-permute-start(f32[3,128,128]{2,1,0:T(8,128)S(1)} %get-tuple-element.15), channel_id=1, source_target_pairs={{2,0},{3,1},{4,2},{5,3},{6,4},{7,5},{8,6},{9,7},{10,8},{11,9},{12,... | collective-permute-start | bytes 589832 | tf_op jit(solution)/shard_map/ppermute | solution.py:12
  156.7 9.3 %collective-permute-start.1 = (f32[3,128,128]{2,1,0:T(8,128)S(1)}, f32[3,128,128]{2,1,0:T(8,128)S(1)}, u32[]{:S(2)}, u32[]{:S(2)}) collective-permute-start(f32[3,128,128]{2,1,0:T(8,128)S(1)} %get-tuple-element.16), channel_id=1, source_target_pairs={{48,0},{72,24},{96,48},{120,72},{144,96},{168,120},{192,144},{216,... | collective-permute-start | bytes 589832 | tf_op jit(solution)/shard_map/ppermute | solution.py:12
  168.4 6.9 %collective-permute-start.25 = (f32[3,128,128]{2,1,0:T(8,128)S(1)}, f32[3,128,128]{2,1,0:T(8,128)S(1)}, u32[]{:S(2)}, u32[]{:S(2)}) collective-permute-start(f32[3,128,128]{2,1,0:T(8,128)S(1)} %get-tuple-element.18), channel_id=1, source_target_pairs={{144,0},{168,24},{192,48},{216,72},{240,96},{264,120},{288,144},{3... | collective-permute-start | bytes 589832 | tf_op jit(solution)/shard_map/ppermute | solution.py:12
  175.4 9.1 %collective-permute-start.8 = (f32[3,128,128]{2,1,0:T(8,128)S(1)}, f32[3,128,128]{2,1,0:T(8,128)}, u32[]{:S(2)}, u32[]{:S(2)}) collective-permute-start(f32[3,128,128]{2,1,0:T(8,128)S(1)} %get-tuple-element.16), channel_id=1, source_target_pairs={{24,0},{48,24},{72,48},{96,72},{120,96},{144,120},{168,144},{192,1... | collective-permute-start | bytes 589832 | tf_op jit(solution)/shard_map/ppermute | solution.py:12
  189.2 10.8 %collective-permute-done.35 = f32[3,128,128]{2,1,0:T(8,128)S(1)} collective-permute-done((f32[3,128,128]{2,1,0:T(8,128)S(1)}, f32[3,128,128]{2,1,0:T(8,128)S(1)}, u32[]{:S(2)}, u32[]{:S(2)}) %collective-permute-start.35) | collective-permute-done | bytes 196640 | tf_op jit(solution)/shard_map/ppermute | solution.py:12
  200.0 8.3 %collective-permute-start.17 = (f32[3,128,128]{2,1,0:T(8,128)}, f32[3,128,128]{2,1,0:T(8,128)S(1)}, u32[]{:S(2)}, u32[]{:S(2)}) collective-permute-start(f32[3,128,128]{2,1,0:T(8,128)} %collective-permute-done.16), channel_id=1, source_target_pairs={{2,0},{3,1},{4,2},{5,3},{6,4},{7,5},{8,6},{9,7},{10,8},{11,9},{12,... | collective-permute-start | bytes 589832 | tf_op jit(solution)/shard_map/ppermute | solution.py:12
  211.1 10.1 %collective-permute-start.5 = (f32[3,128,128]{2,1,0:T(8,128)}, f32[3,128,128]{2,1,0:T(8,128)S(1)}, u32[]{:S(2)}, u32[]{:S(2)}) collective-permute-start(f32[3,128,128]{2,1,0:T(8,128)} %collective-permute-done.4), channel_id=1, source_target_pairs={{1,0},{2,1},{3,2},{4,3},{5,4},{6,5},{7,6},{8,7},{9,8},{10,9},{11,1... | collective-permute-start | bytes 589832 | tf_op jit(solution)/shard_map/ppermute | solution.py:12
  225.1 5.7 %collective-permute-start.33 = (f32[3,128,128]{2,1,0:T(8,128)}, f32[3,128,128]{2,1,0:T(8,128)S(1)}, u32[]{:S(2)}, u32[]{:S(2)}) collective-permute-start(f32[3,128,128]{2,1,0:T(8,128)} %collective-permute-done.32), channel_id=1, source_target_pairs={{3,0},{4,1},{5,2},{6,3},{7,4},{8,5},{9,6},{10,7},{11,8},{12,9},{13... | collective-permute-start | bytes 589832 | tf_op jit(solution)/shard_map/ppermute | solution.py:12
  232.2 4.9 %collective-permute-done.5 = f32[3,128,128]{2,1,0:T(8,128)S(1)} collective-permute-done((f32[3,128,128]{2,1,0:T(8,128)}, f32[3,128,128]{2,1,0:T(8,128)S(1)}, u32[]{:S(2)}, u32[]{:S(2)}) %collective-permute-start.5) | collective-permute-done | bytes 196640 | tf_op jit(solution)/shard_map/ppermute | solution.py:12
  237.1 9.5 %collective-permute-done.9 = f32[3,128,128]{2,1,0:T(8,128)S(1)} collective-permute-done((f32[3,128,128]{2,1,0:T(8,128)}, f32[3,128,128]{2,1,0:T(8,128)S(1)}, u32[]{:S(2)}, u32[]{:S(2)}) %collective-permute-start.9) | collective-permute-done | bytes 196640 | tf_op jit(solution)/shard_map/ppermute | solution.py:12
  248.1 30.3 %collective-permute-done.29 = f32[3,128,128]{2,1,0:T(8,128)S(1)} collective-permute-done((f32[3,128,128]{2,1,0:T(8,128)}, f32[3,128,128]{2,1,0:T(8,128)S(1)}, u32[]{:S(2)}, u32[]{:S(2)}) %collective-permute-start.29) | collective-permute-done | bytes 196640 | tf_op jit(solution)/shard_map/ppermute | solution.py:12
  (69 shorter events, 51.8 us)
Async XLA Ops:
  1.2 35.2 %collective-permute-start.22 = (s32[3]{0:T(128)S(1)}, s32[3]{0:T(128)S(1)}, u32[]{:S(2)}, u32[]{:S(2)}) collective-permute-start(s32[3]{0:T(128)S(1)} %get-tuple-element.6), channel_id=1, source_target_pairs={{4,0},{5,1},{6,2},{7,3},{8,4},{9,5},{10,6},{11,7},{12,8},{13,9},{1... | collective-permute-start | bytes 44 | tf_op jit(solution)/shard_map/ppermute | solution.py:12
  4.2 63.4 %collective-permute-start.14 = (s32[3]{0:T(128)S(1)}, s32[3]{0:T(128)S(1)}, u32[]{:S(2)}, u32[]{:S(2)}) collective-permute-start(s32[3]{0:T(128)S(1)} %get-tuple-element.6), channel_id=1, source_target_pairs={{48,0},{72,24},{96,48},{120,72},{144,96},{168,120},{192,144},{216,... | collective-permute-start | bytes 44 | tf_op jit(solution)/shard_map/ppermute | solution.py:12
  20.9 50.2 %collective-permute-start.18 = (s32[3]{0:T(128)S(1)}, s32[3]{0:T(128)S(1)}, u32[]{:S(2)}, u32[]{:S(2)}) collective-permute-start(s32[3]{0:T(128)S(1)} %get-tuple-element.7), channel_id=1, source_target_pairs={{48,0},{72,24},{96,48},{120,72},{144,96},{168,120},{192,144},{216,... | collective-permute-start | bytes 44 | tf_op jit(solution)/shard_map/ppermute | solution.py:12
  23.7 17.4 %collective-permute-start.12 = (s32[3]{0:T(128)S(1)}, s32[3]{0:T(128)S(1)}, u32[]{:S(2)}, u32[]{:S(2)}) collective-permute-start(s32[3]{0:T(128)S(1)} %get-tuple-element.7), channel_id=1, source_target_pairs={{96,0},{120,24},{144,48},{168,72},{192,96},{216,120},{240,144},{26... | collective-permute-start | bytes 44 | tf_op jit(solution)/shard_map/ppermute | solution.py:12
  26.1 19.0 %collective-permute-start.10 = (s32[3]{0:T(128)S(1)}, s32[3]{0:T(128)S(1)}, u32[]{:S(2)}, u32[]{:S(2)}) collective-permute-start(s32[3]{0:T(128)S(1)} %get-tuple-element.8), channel_id=1, source_target_pairs={{2,0},{3,1},{4,2},{5,3},{6,4},{7,5},{8,6},{9,7},{10,8},{11,9},{12,... | collective-permute-start | bytes 44 | tf_op jit(solution)/shard_map/ppermute | solution.py:12
  36.5 58.1 %collective-permute-start.2 = (s32[3]{0:T(128)S(1)}, s32[3]{0:T(128)S(1)}, u32[]{:S(2)}, u32[]{:S(2)}) collective-permute-start(s32[3]{0:T(128)S(1)} %get-tuple-element.8), channel_id=1, source_target_pairs={{24,0},{48,24},{72,48},{96,72},{120,96},{144,120},{168,144},{192,1... | collective-permute-start | bytes 44 | tf_op jit(solution)/shard_map/ppermute | solution.py:12
  41.0 55.5 %collective-permute-start.6 = (s32[3]{0:T(128)S(1)}, s32[3]{0:T(128)S(1)}, u32[]{:S(2)}, u32[]{:S(2)}) collective-permute-start(s32[3]{0:T(128)S(1)} %get-tuple-element.9), channel_id=1, source_target_pairs={{24,0},{48,24},{72,48},{96,72},{120,96},{144,120},{168,144},{192,1... | collective-permute-start | bytes 44 | tf_op jit(solution)/shard_map/ppermute | solution.py:12
  50.5 8.4 %collective-permute-start.34 = (s32[3]{0:T(128)S(1)}, s32[3]{0:T(128)S(1)}, u32[]{:S(2)}, u32[]{:S(2)}) collective-permute-start(s32[3]{0:T(128)S(1)} %get-tuple-element.10), channel_id=1, source_target_pairs={{6,0},{7,1},{8,2},{9,3},{10,4},{11,5},{12,6},{13,7},{14,8},{15,9},... | collective-permute-start | bytes 44 | tf_op jit(solution)/shard_map/ppermute | solution.py:12
  65.6 48.8 %collective-permute-start.26 = (s32[3]{0:T(128)S(1)}, s32[3]{0:T(128)S(1)}, u32[]{:S(2)}, u32[]{:S(2)}) collective-permute-start(s32[3]{0:T(128)S(1)} %get-tuple-element.10), channel_id=1, source_target_pairs={{72,0},{96,24},{120,48},{144,72},{168,96},{192,120},{216,144},{240... | collective-permute-start | bytes 44 | tf_op jit(solution)/shard_map/ppermute | solution.py:12
  67.6 87.2 %collective-permute-start.23 = (f32[3,128,128]{2,1,0:T(8,128)S(1)}, f32[3,128,128]{2,1,0:T(8,128)S(1)}, u32[]{:S(2)}, u32[]{:S(2)}) collective-permute-start(f32[3,128,128]{2,1,0:T(8,128)S(1)} %get-tuple-element.13), channel_id=1, source_target_pairs={{4,0},{5,1},{6,2},{7,3},{8,4},{9,5},{10,6},{11,7},{12,8},{13,9},{1... | collective-permute-start | bytes 589832 | tf_op jit(solution)/shard_map/ppermute | solution.py:12
  77.4 7.2 %collective-permute-start.19 = (s32[3]{0:T(128)S(1)}, s32[3]{0:T(128)S(1)}, u32[]{:S(2)}, u32[]{:S(2)}) collective-permute-start(s32[3]{0:T(128)S(1)} %collective-permute-done.18), channel_id=1, source_target_pairs={{2,0},{3,1},{4,2},{5,3},{6,4},{7,5},{8,6},{9,7},{10,8},{11,9},{12,... | collective-permute-start | bytes 44 | tf_op jit(solution)/shard_map/ppermute | solution.py:12
  84.6 72.1 %collective-permute-start.16 = (f32[3,128,128]{2,1,0:T(8,128)S(1)}, f32[3,128,128]{2,1,0:T(8,128)}, u32[]{:S(2)}, u32[]{:S(2)}) collective-permute-start(f32[3,128,128]{2,1,0:T(8,128)S(1)} %get-tuple-element.13), channel_id=1, source_target_pairs={{48,0},{72,24},{96,48},{120,72},{144,96},{168,120},{192,144},{216,... | collective-permute-start | bytes 589832 | tf_op jit(solution)/shard_map/ppermute | solution.py:12
  94.6 71.5 %collective-permute-start.20 = (f32[3,128,128]{2,1,0:T(8,128)S(1)}, f32[3,128,128]{2,1,0:T(8,128)}, u32[]{:S(2)}, u32[]{:S(2)}) collective-permute-start(f32[3,128,128]{2,1,0:T(8,128)S(1)} %get-tuple-element.14), channel_id=1, source_target_pairs={{48,0},{72,24},{96,48},{120,72},{144,96},{168,120},{192,144},{216,... | collective-permute-start | bytes 589832 | tf_op jit(solution)/shard_map/ppermute | solution.py:12
  96.5 9.0 %collective-permute-start.3 = (s32[3]{0:T(128)S(1)}, s32[3]{0:T(128)S(1)}, u32[]{:S(2)}, u32[]{:S(2)}) collective-permute-start(s32[3]{0:T(128)S(1)} %collective-permute-done.2), channel_id=1, source_target_pairs={{1,0},{2,1},{3,2},{4,3},{5,4},{6,5},{7,6},{8,7},{9,8},{10,9},{11,1... | collective-permute-start | bytes 44 | tf_op jit(solution)/shard_map/ppermute | solution.py:12
  111.0 57.4 %collective-permute-start.13 = (f32[3,128,128]{2,1,0:T(8,128)S(1)}, f32[3,128,128]{2,1,0:T(8,128)S(1)}, u32[]{:S(2)}, u32[]{:S(2)}) collective-permute-start(f32[3,128,128]{2,1,0:T(8,128)S(1)} %get-tuple-element.14), channel_id=1, source_target_pairs={{96,0},{120,24},{144,48},{168,72},{192,96},{216,120},{240,144},{26... | collective-permute-start | bytes 589832 | tf_op jit(solution)/shard_map/ppermute | solution.py:12
  114.4 18.0 %collective-permute-start.30 = (s32[3]{0:T(128)S(1)}, s32[3]{0:T(128)S(1)}, u32[]{:S(2)}, u32[]{:S(2)}) collective-permute-start(s32[3]{0:T(128)S(1)} %get-tuple-element.11), channel_id=1, source_target_pairs={{72,0},{96,24},{120,48},{144,72},{168,96},{192,120},{216,144},{240... | collective-permute-start | bytes 44 | tf_op jit(solution)/shard_map/ppermute | solution.py:12
  132.4 9.3 %collective-permute-start.27 = (s32[3]{0:T(128)S(1)}, s32[3]{0:T(128)S(1)}, u32[]{:S(2)}, u32[]{:S(2)}) collective-permute-start(s32[3]{0:T(128)S(1)} %collective-permute-done.26), channel_id=1, source_target_pairs={{3,0},{4,1},{5,2},{6,3},{7,4},{8,5},{9,6},{10,7},{11,8},{12,9},{13... | collective-permute-start | bytes 44 | tf_op jit(solution)/shard_map/ppermute | solution.py:12
  141.7 9.3 %collective-permute-start.31 = (s32[3]{0:T(128)S(1)}, s32[3]{0:T(128)S(1)}, u32[]{:S(2)}, u32[]{:S(2)}) collective-permute-start(s32[3]{0:T(128)S(1)} %collective-permute-done.30), channel_id=1, source_target_pairs={{3,0},{4,1},{5,2},{6,3},{7,4},{8,5},{9,6},{10,7},{11,8},{12,9},{13... | collective-permute-start | bytes 44 | tf_op jit(solution)/shard_map/ppermute | solution.py:12
  151.0 24.3 %collective-permute-start.11 = (f32[3,128,128]{2,1,0:T(8,128)S(1)}, f32[3,128,128]{2,1,0:T(8,128)S(1)}, u32[]{:S(2)}, u32[]{:S(2)}) collective-permute-start(f32[3,128,128]{2,1,0:T(8,128)S(1)} %get-tuple-element.15), channel_id=1, source_target_pairs={{2,0},{3,1},{4,2},{5,3},{6,4},{7,5},{8,6},{9,7},{10,8},{11,9},{12,... | collective-permute-start | bytes 589832 | tf_op jit(solution)/shard_map/ppermute | solution.py:12
  154.8 29.7 %collective-permute-start.4 = (f32[3,128,128]{2,1,0:T(8,128)S(1)}, f32[3,128,128]{2,1,0:T(8,128)}, u32[]{:S(2)}, u32[]{:S(2)}) collective-permute-start(f32[3,128,128]{2,1,0:T(8,128)S(1)} %get-tuple-element.15), channel_id=1, source_target_pairs={{24,0},{48,24},{72,48},{96,72},{120,96},{144,120},{168,144},{192,1... | collective-permute-start | bytes 589832 | tf_op jit(solution)/shard_map/ppermute | solution.py:12
  156.7 30.3 %collective-permute-start.1 = (f32[3,128,128]{2,1,0:T(8,128)S(1)}, f32[3,128,128]{2,1,0:T(8,128)S(1)}, u32[]{:S(2)}, u32[]{:S(2)}) collective-permute-start(f32[3,128,128]{2,1,0:T(8,128)S(1)} %get-tuple-element.16), channel_id=1, source_target_pairs={{48,0},{72,24},{96,48},{120,72},{144,96},{168,120},{192,144},{216,... | collective-permute-start | bytes 589832 | tf_op jit(solution)/shard_map/ppermute | solution.py:12
  166.1 33.9 %collective-permute-start.35 = (f32[3,128,128]{2,1,0:T(8,128)S(1)}, f32[3,128,128]{2,1,0:T(8,128)S(1)}, u32[]{:S(2)}, u32[]{:S(2)}) collective-permute-start(f32[3,128,128]{2,1,0:T(8,128)S(1)} %get-tuple-element.17), channel_id=1, source_target_pairs={{6,0},{7,1},{8,2},{9,3},{10,4},{11,5},{12,6},{13,7},{14,8},{15,9},... | collective-permute-start | bytes 589832 | tf_op jit(solution)/shard_map/ppermute | solution.py:12
  168.4 39.9 %collective-permute-start.25 = (f32[3,128,128]{2,1,0:T(8,128)S(1)}, f32[3,128,128]{2,1,0:T(8,128)S(1)}, u32[]{:S(2)}, u32[]{:S(2)}) collective-permute-start(f32[3,128,128]{2,1,0:T(8,128)S(1)} %get-tuple-element.18), channel_id=1, source_target_pairs={{144,0},{168,24},{192,48},{216,72},{240,96},{264,120},{288,144},{3... | collective-permute-start | bytes 589832 | tf_op jit(solution)/shard_map/ppermute | solution.py:12
  175.4 35.7 %collective-permute-start.8 = (f32[3,128,128]{2,1,0:T(8,128)S(1)}, f32[3,128,128]{2,1,0:T(8,128)}, u32[]{:S(2)}, u32[]{:S(2)}) collective-permute-start(f32[3,128,128]{2,1,0:T(8,128)S(1)} %get-tuple-element.16), channel_id=1, source_target_pairs={{24,0},{48,24},{72,48},{96,72},{120,96},{144,120},{168,144},{192,1... | collective-permute-start | bytes 589832 | tf_op jit(solution)/shard_map/ppermute | solution.py:12
  184.5 36.7 %collective-permute-start.28 = (f32[3,128,128]{2,1,0:T(8,128)S(1)}, f32[3,128,128]{2,1,0:T(8,128)}, u32[]{:S(2)}, u32[]{:S(2)}) collective-permute-start(f32[3,128,128]{2,1,0:T(8,128)S(1)} %get-tuple-element.17), channel_id=1, source_target_pairs={{72,0},{96,24},{120,48},{144,72},{168,96},{192,120},{216,144},{240... | collective-permute-start | bytes 589832 | tf_op jit(solution)/shard_map/ppermute | solution.py:12
  187.1 36.0 %collective-permute-start.32 = (f32[3,128,128]{2,1,0:T(8,128)S(1)}, f32[3,128,128]{2,1,0:T(8,128)}, u32[]{:S(2)}, u32[]{:S(2)}) collective-permute-start(f32[3,128,128]{2,1,0:T(8,128)S(1)} %get-tuple-element.18), channel_id=1, source_target_pairs={{72,0},{96,24},{120,48},{144,72},{168,96},{192,120},{216,144},{240... | collective-permute-start | bytes 589832 | tf_op jit(solution)/shard_map/ppermute | solution.py:12
  200.0 25.0 %collective-permute-start.17 = (f32[3,128,128]{2,1,0:T(8,128)}, f32[3,128,128]{2,1,0:T(8,128)S(1)}, u32[]{:S(2)}, u32[]{:S(2)}) collective-permute-start(f32[3,128,128]{2,1,0:T(8,128)} %collective-permute-done.16), channel_id=1, source_target_pairs={{2,0},{3,1},{4,2},{5,3},{6,4},{7,5},{8,6},{9,7},{10,8},{11,9},{12,... | collective-permute-start | bytes 589832 | tf_op jit(solution)/shard_map/ppermute | solution.py:12
  208.3 22.5 %collective-permute-start.21 = (f32[3,128,128]{2,1,0:T(8,128)}, f32[3,128,128]{2,1,0:T(8,128)S(1)}, u32[]{:S(2)}, u32[]{:S(2)}) collective-permute-start(f32[3,128,128]{2,1,0:T(8,128)} %collective-permute-done.20), channel_id=1, source_target_pairs={{2,0},{3,1},{4,2},{5,3},{6,4},{7,5},{8,6},{9,7},{10,8},{11,9},{12,... | collective-permute-start | bytes 589832 | tf_op jit(solution)/shard_map/ppermute | solution.py:12
  211.1 26.1 %collective-permute-start.5 = (f32[3,128,128]{2,1,0:T(8,128)}, f32[3,128,128]{2,1,0:T(8,128)S(1)}, u32[]{:S(2)}, u32[]{:S(2)}) collective-permute-start(f32[3,128,128]{2,1,0:T(8,128)} %collective-permute-done.4), channel_id=1, source_target_pairs={{1,0},{2,1},{3,2},{4,3},{5,4},{6,5},{7,6},{8,7},{9,8},{10,9},{11,1... | collective-permute-start | bytes 589832 | tf_op jit(solution)/shard_map/ppermute | solution.py:12
  221.2 25.5 %collective-permute-start.9 = (f32[3,128,128]{2,1,0:T(8,128)}, f32[3,128,128]{2,1,0:T(8,128)S(1)}, u32[]{:S(2)}, u32[]{:S(2)}) collective-permute-start(f32[3,128,128]{2,1,0:T(8,128)} %collective-permute-done.8), channel_id=1, source_target_pairs={{1,0},{2,1},{3,2},{4,3},{5,4},{6,5},{7,6},{8,7},{9,8},{10,9},{11,1... | collective-permute-start | bytes 589832 | tf_op jit(solution)/shard_map/ppermute | solution.py:12
  223.1 55.2 %collective-permute-start.29 = (f32[3,128,128]{2,1,0:T(8,128)}, f32[3,128,128]{2,1,0:T(8,128)S(1)}, u32[]{:S(2)}, u32[]{:S(2)}) collective-permute-start(f32[3,128,128]{2,1,0:T(8,128)} %collective-permute-done.28), channel_id=1, source_target_pairs={{3,0},{4,1},{5,2},{6,3},{7,4},{8,5},{9,6},{10,7},{11,8},{12,9},{13... | collective-permute-start | bytes 589832 | tf_op jit(solution)/shard_map/ppermute | solution.py:12
  225.1 55.4 %collective-permute-start.33 = (f32[3,128,128]{2,1,0:T(8,128)}, f32[3,128,128]{2,1,0:T(8,128)S(1)}, u32[]{:S(2)}, u32[]{:S(2)}) collective-permute-start(f32[3,128,128]{2,1,0:T(8,128)} %collective-permute-done.32), channel_id=1, source_target_pairs={{3,0},{4,1},{5,2},{6,3},{7,4},{8,5},{9,6},{10,7},{11,8},{12,9},{13... | collective-permute-start | bytes 589832 | tf_op jit(solution)/shard_map/ppermute | solution.py:12
  (4 other events, 23.8 us)
where the time goes:
time: 285 us; the launch traced here: 284 us
  starting transfers between devices  163 us (57%)
  waiting for transfers between devices  108 us (38%)
  local copies, waits for them, and re-layouts  5.7 us (2%)
  matrix products  5.68 us (2%)
    ppermute x36, starting transfers between devices, passed_along(): return lax.ppermute(block, axis, route)  163 us
    ppermute x36, waiting for transfers between devices, passed_along(): return lax.ppermute(block, axis, route)  108 us
  transfers between devices with their start and end apart: 36, of which 15 were waited for; matrix products, arithmetic and copies ran while one was open for 3% of the time, Pallas kernels for 0%

commit v1 on v0

v1 whole, which is shorter than its diff:
```python
import functools

import jax
import jax.numpy as jnp
from jax import lax
from jax.experimental import pallas as pl
from jax.experimental.pallas import tpu as pltpu
from jax.sharding import PartitionSpec as P

MESH = pl.DeviceIdType.MESH
BS = 128
TAU = 3
STEPS = 4
N_ROW = 32
N_COL = 24
HEIGHT = TAU * BS + 8

RING = 8


def straight(k, m):
    return (
        lambda r, c: ((r + N_ROW - k) % N_ROW, (c + N_COL - m) % N_COL),
        lambda r, c: ((r + N_ROW + k) % N_ROW, (c + N_COL + m) % N_COL),
    )


def around(at, k):
    return at - at % RING + (at % RING + RING - k) % RING


def in_plane(k, m):
    return lambda r, c: (around(r, k), around(c, m)), lambda r, c: (around(r, -k), around(c, -m))


def in_row_plane(k, m):
    return (
        lambda r, c: (around(r, k), (c + N_COL - m) % N_COL),
        lambda r, c: (around(r, -k), (c + m) % N_COL),
    )


def wrapped(at, k):
    return jnp.where(at % RING >= RING - k, RING, 0)


def down(k, m):
    return (
        lambda r, c: ((r + N_ROW - wrapped(r, k)) % N_ROW, (c + N_COL - wrapped(c, m)) % N_COL),
        lambda r, c: ((r + wrapped(r, k)) % N_ROW, (c + wrapped(c, m)) % N_COL),
    )


class Leg:
    def __init__(self, name, src, move, sends=None):
        self.name, self.src, self.sends = name, src, sends
        self.to, self.origin = move
        self.gets = None if sends is None else lambda r, c: sends(*self.origin(r, c))


def plan():
    legs, final = [], {}

    def late(name, src, k, m):
        crossed = lambda r, c: (r % RING >= RING - k) | (c % RING >= RING - m)
        legs.append(Leg(name, src, in_plane(k, m)))
        return Leg(name + "z", name, down(k, m), crossed), (crossed, name + "z", name)

    def shared(s):
        low = lambda k: lambda r, c: r % RING < k
        legs.append(Leg(f"f{s}", f"F{s}", straight(RING, 0), low(2 * s)))
        return [
            Leg(f"fe{s}", (low(2 * s), f"f{s}", f"F{s}"), in_plane(2 * s, 0)),
            Leg(f"fm{s}", (low(s), f"f{s}", f"F{s}"), in_row_plane(s, s)),
        ]

    f3 = shared(3)
    f2 = shared(2)
    bm2, bm2_at = late("bm2", "B2", 2, 2)
    bs2, bs2_at = late("bs2", "B2", 0, 4)
    fe1, fe1_at = late("fe1", "F1", 2, 0)
    fm1, fm1_at = late("fm1", "F1", 1, 1)
    bm1, bm1_at = late("bm1", "B1", 1, 1)
    legs += [Leg("bs3", "B3", straight(0, 6)), Leg("bs1", "B1", straight(0, 2))]
    legs += [fe1, fm1, bm1, bm2, bs2] + f2 + f3 + [Leg("bm3", "bs3", straight(3, -3))]
    final[1] = fm1_at, "bs1", fe1_at, bm1_at
    final[2] = "fm2", bs2_at, "fe2", bm2_at
    final[3] = "fm3", "bs3", "fe3", "bm3"
    return legs, final


OWN = ["F1", "F2", "F3", "B1", "B2", "B3"]


def places(legs):
    return {name: at for at, name in enumerate(OWN + [leg.name for leg in legs])}


def pick(src, at, r, c):
    if isinstance(src, str):
        return at[src]
    condition, yes, no = src
    return jnp.where(condition(r, c), at[yes], at[no])


def names(src):
    return {src} if isinstance(src, str) else set(src[1:])


def when(condition, r, c, do):
    if condition is None:
        do()
    else:
        pl.when(condition(r, c))(do)


def split(value):
    high = value.astype(jnp.bfloat16)
    return high, (value - high.astype(jnp.float32)).astype(jnp.bfloat16)


def dot(a, b):
    return jnp.dot(a, b, preferred_element_type=jnp.float32)


def kernel(legs, final, u_ref, rows_ref, out_ref, buf, onsite, lefts, rights, result, load_sem, store_sem, send_sem, recv_sem):
    r, c = lax.axis_index("row"), lax.axis_index("col")
    at = places(legs)
    copies = {}
    for number, leg in enumerate(legs):
        copies[leg.name] = pltpu.make_async_remote_copy(
            src_ref=buf.at[pick(leg.src, at, r, c)],
            dst_ref=buf.at[at[leg.name]],
            send_sem=send_sem.at[number],
            recv_sem=recv_sem.at[number],
            device_id=leg.to(r, c),
            device_id_type=MESH,
        )

    barrier = pltpu.get_barrier_semaphore()
    partners = 0
    for leg in legs:
        greet = functools.partial(
            pl.semaphore_signal, barrier, inc=1, device_id=leg.origin(r, c), device_id_type=MESH
        )
        when(leg.gets, r, c, greet)
        partners += 1 if leg.sends is None else jnp.where(leg.sends(r, c), 1, 0)

    loads = []
    for j in range(2 * STEPS - 1):
        for t in range(TAU):
            target = onsite.at[t] if j == 0 else buf.at[j - 1, pl.ds(t * BS, BS)]
            loads.append(pltpu.make_async_copy(u_ref.at[t, j], target, load_sem.at[j, t]))
            loads[-1].start()
    for j in range(1, 2 * STEPS - 1):
        label = jnp.concatenate(
            [jnp.full((1, BS), rows_ref[t, j], jnp.int32) for t in range(TAU)] + [jnp.zeros((8 - TAU, BS), jnp.int32)]
        )
        buf[j - 1, TAU * BS : HEIGHT, :] = label.astype(jnp.float32)
    for load in loads:
        load.wait()
    pl.semaphore_wait(barrier, partners)

    for leg in legs:
        if leg.src in OWN:
            when(leg.sends, r, c, copies[leg.name].start)
        elif not isinstance(leg.src, str) and leg.src[2] in OWN:
            when(lambda r, c: jnp.logical_not(leg.src[0](r, c)), r, c, copies[leg.name].start)

    def put(side, i, k, value):
        high, low = split(value)
        side[0, i * BS : (i + 1) * BS, k * BS : (k + 1) * BS] = high
        side[1, i * BS : (i + 1) * BS, k * BS : (k + 1) * BS] = low

    def chosen(label, k, block):
        return jnp.where(label == float(k), block, 0.0)

    def assemble(side, forward, forward_labels, backward, backward_labels):
        for i in range(TAU):
            turned = backward(i).T
            for k in range(TAU):
                put(side, i, k, chosen(forward_labels(k), i, forward(k)) + chosen(backward_labels(i), k, turned))

    def multiply(s, left, right):
        for i in range(TAU):
            rows = slice(i * BS, (i + 1) * BS)
            high = left[0, rows, :]
            total = dot(high, right[1]) + dot(left[1, rows, :], right[0]) + dot(high, right[0])
            for j in range(TAU):
                result[s, i, j] = total[:, j * BS : (j + 1) * BS]
        store = pltpu.make_async_copy(result.at[s], out_ref.at[s], store_sem.at[s])
        store.start()
        return store

    own_labels = lambda t: jnp.full((1, BS), rows_ref[t, 0], jnp.int32).astype(jnp.float32)
    own_block = lambda t: onsite[t]
    assemble(lefts, own_block, own_labels, own_block, own_labels)
    stores = [multiply(0, lefts, lefts)]

    def parts_of(src):
        place = pick(src, at, r, c)
        block = lambda t: buf[place, t * BS : (t + 1) * BS, :]
        labels = lambda t: buf[place, TAU * BS + t : TAU * BS + t + 1, :]
        return block, labels

    arrived = set(OWN)
    for leg in legs:
        when(leg.gets, r, c, copies[leg.name].wait_recv)
        arrived.add(leg.name)
        for later in legs:
            if leg.name in names(later.src):
                if isinstance(later.src, str):
                    when(later.sends, r, c, copies[later.name].start)
                else:
                    when(later.src[0], r, c, copies[later.name].start)
        for s in range(1, STEPS):
            needs = set().union(*(names(src) for src in final[s]))
            if leg.name in needs and arrived >= needs:
                fm, bs, fe, bm = (parts_of(src) for src in final[s])
                assemble(lefts, *fm, *bs)
                assemble(rights, *fe, *bm)
                stores.append(multiply(s, lefts, rights))
    for leg in legs:
        when(leg.sends, r, c, copies[leg.name].wait_send)
    for store in stores:
        store.wait()


def shards(u_blocks, u_rows):
    legs, final = plan()
    count = len(OWN) + len(legs)
    return pl.pallas_call(
        functools.partial(kernel, legs, final),
        out_shape=jax.ShapeDtypeStruct((STEPS, TAU, TAU, BS, BS), jnp.float32),
        in_specs=[pl.BlockSpec(memory_space=pl.ANY), pl.BlockSpec(memory_space=pltpu.SMEM)],
        out_specs=pl.BlockSpec(memory_space=pl.ANY),
        scratch_shapes=[
            pltpu.VMEM((count, HEIGHT, BS), jnp.float32),
            pltpu.VMEM((TAU, BS, BS), jnp.float32),
            pltpu.VMEM((2, TAU * BS, TAU * BS), jnp.bfloat16),
            pltpu.VMEM((2, TAU * BS, TAU * BS), jnp.bfloat16),
            pltpu.VMEM((STEPS, TAU, TAU, BS, BS), jnp.float32),
            pltpu.SemaphoreType.DMA((2 * STEPS - 1, TAU)),
            pltpu.SemaphoreType.DMA((STEPS,)),
            pltpu.SemaphoreType.DMA((len(legs),)),
            pltpu.SemaphoreType.DMA((len(legs),)),
        ],
        compiler_params=pltpu.CompilerParams(collective_id=0, has_side_effects=True, vmem_limit_bytes=48 << 20),
    )(u_blocks, u_rows)


def solution(mesh):
    return jax.shard_map(
        shards,
        mesh=mesh,
        in_specs=(P("row", "col", None, None), P("row", "col")),
        out_specs=P("row", "col", None, None, None),
        check_vma=False,
    )
```

time: 285 us -> 109 us (0.38)
  the two profiles are of different devices: /device:TPU:40 before, /device:TPU:19 now
where the time goes in v1:
time: 109 us
  Pallas kernels  106 us (97%)
  local copies, waits for them, and re-layouts  3.43 us (3%)
    pallas_call x1, Pallas kernels, shards(): pl.pallas_call(functools.partial(kernel, legs, final), out_shape=jax.Shap...  106 us
    unnamed x5, local copies, waits for them, and re-layouts  3.43 us

profile of v1, /device:TPU:19, one launch (start us, length us, event | category | flops | bytes accessed | tf_op | source)
XLA Modules:
  0.0 109.3 jit_solution(4793138802037278628)
XLA Ops:
  0.0 0.0 copy-start
  0.0 1.3 %copy-done = f32[3,7,128,128]{3,2,1,0:T(8,128)S(1)} copy-done((f32[3,7,128,128]{3,2,1,0:T(8,128)S(1)}, f32[3,7,128,128]{3,2,1,0:T(8,128)}, u32[]{:S(2)}) %copy-start) | copy-done | bytes 1376280
  1.3 0.0 copy-start.1
  1.3 0.7 copy-done.1
  2.0 105.8 %shard_map.28 = f32[4,3,3,128,128]{4,3,2,1,0:T(8,128)S(1)} custom-call(f32[3,7,128,128]{3,2,1,0:T(8,128)S(1)} %copy-done, s32[3,7]{1,0:T(4,128)S(1)} %copy-done.1), custom_call_target="tpu_custom_call" | custom-call | tf_op jit(solution)/shard_map/pallas_call | solution.py:232
  107.8 1.4 %copy.4 = f32[4,3,3,128,128]{4,3,2,1,0:T(8,128)} copy(f32[4,3,3,128,128]{4,3,2,1,0:T(8,128)S(1)} %shard_map.28) | data formatting | bytes 4718592
Async XLA Ops:
  0.0 1.3 %copy-start = (f32[3,7,128,128]{3,2,1,0:T(8,128)S(1)}, f32[3,7,128,128]{3,2,1,0:T(8,128)}, u32[]{:S(2)}) copy-start(f32[3,7,128,128]{3,2,1,0:T(8,128)} %u_ref.1) | copy-start | bytes 4128772
  1.3 0.7 copy-start.1
